TPU v7x, 128 devices: a whole 4x4x4 slice. The times are simulated.
128 devices in a mesh: dev: 128 (over y, z, x, core).
Axes of the slice: x: 4, y: 4, z: 4, core: 2. Of those that a mesh axis runs over, the one named last changes fastest.
Arguments:
- runs_field: float32 [2048, 256, 256], P('dev'), may hold values from -6 to 6
- spectral_filter: float32 [256, 129], replicated, may hold values from 0.3 to 3, as said below
- block_inverses: float32 [2, 256, 256], replicated, may hold values from -1.5 to 1.5, as said below
- factor_panels: float32 [2, 2048, 256], P(None, 'dev'), may hold values from -0.375 to 0.375
Outputs:
- solved: float32 [2048, 65536], P(None, 'dev')
Inputs may be any that keep to these rules, and one draw needn't show every extreme that they name: `spectral_filter`: symmetric under the first frequency index k -> (256 - k) mod 256 in columns 0 and 128. `block_inverses`: each block is lower triangular with diagonal entries from 0.7 to 1.4.
All inputs are finite; a program needn't handle non-finite values.
Results may differ from a plain program's by a relative error of at most 0.000076.
Values sent between devices are 32-bit elements; how exact they have to be, the bound alone decides.
A program may use at most 64 MiB of HBM per device.

v0:
```python
import math

import jax
import jax.numpy as jnp
import numpy as np
from jax import lax
from jax.experimental import pallas as pl
from jax.experimental.pallas import tpu as pltpu
from jax.sharding import PartitionSpec as P

MESH = pl.DeviceIdType.MESH
F32, BF16 = jnp.float32, jnp.bfloat16
N, HALF = 256, 128
DEVS = 128
GROUP = 4


def tables():
    n = np.arange(N)[:, None]
    k = np.arange(HALF)[None, :]
    angle = 2.0 * math.pi * ((n * k) % N) / N
    low = np.sin(angle)
    low[:, 0] = np.where(np.arange(N) % 2 == 0, 1.0, -1.0)
    v = np.concatenate([np.cos(angle), low], axis=1).astype(np.float32)
    high = v.astype(jnp.bfloat16)
    rest = (v - high.astype(np.float32)).astype(jnp.bfloat16)
    return np.stack([high, rest, high.T, rest.T])


def split(value):
    high = value.astype(BF16)
    return high, (value - high.astype(F32)).astype(BF16)


def dot(a, b):
    return jnp.dot(a, b, preferred_element_type=F32)


def dot3(a, b):
    return dot(a[0], b[0]) + (dot(a[0], b[1]) + dot(a[1], b[0]))


def coefficients(filter_t):
    row = lax.broadcasted_iota(jnp.int32, (HALF, N), 0)
    col = lax.broadcasted_iota(jnp.int32, (HALF, N), 1)
    same = (row == col).astype(F32)
    other = ((row + col == N) & (row > 0)).astype(F32)
    nyquist = ((row == 0) & (col == HALF)).astype(F32)
    not_zero = (row > 0).astype(F32)
    picks = [same + other, (same + other) * not_zero + nyquist, (same - other) * not_zero]
    pick = jnp.concatenate(picks, axis=0).astype(BF16)
    one = filter_t.astype(BF16)
    left = filter_t - one.astype(F32)
    two = left.astype(BF16)
    three = (left - two.astype(F32)).astype(BF16)

    def take(part):
        return lax.dot_general(pick, part, (((1,), (1,)), ((), ())), preferred_element_type=F32)

    mixed = (take(three) + take(two)) + take(one)
    lane = lax.broadcasted_iota(jnp.int32, (3 * HALF, HALF), 1)
    scale = jnp.where(lane == 0, 1.0, 2.0).astype(F32) / float(N * N)
    p = mixed[:, :HALF]
    q = jnp.where(lane == 0, mixed[:, HALF : HALF + 1], p)
    p, q = p * scale, q * scale
    even = jnp.concatenate([p[: 2 * HALF], q[: 2 * HALF]], axis=1)
    odd_p, odd_q = p[2 * HALF :], q[2 * HALF :]
    odd = jnp.concatenate(
        [jnp.concatenate([-odd_q, odd_p], axis=1), jnp.concatenate([odd_q, -odd_p], axis=1)], axis=0
    )
    return even, odd


def front_kernel(
    x_hbm, filt_hbm, inv_hbm, pan_hbm, tab_hbm, land, gh_hbm, gl_hbm,
    x, filt, inv, tab, even, odd, out, gath, pan, gh, gl,
    xsem, csem, psem, gsem, a_send, a_recv, g_send, g_recv, lsem,
):
    me = lax.axis_index("dev")
    y, z, xx, c = me // 32, (me // 8) % 4, (me // 2) % 4, me % 2
    partner = me + 1 - 2 * c
    bar = pltpu.get_barrier_semaphore()

    def greet(k, carry):
        pl.semaphore_signal(bar, inc=1, device_id=(lax.rem(me + k, DEVS),), device_id_type=MESH)
        return carry

    def place(u, core, cx, cz, cy):
        rot = (core * 4 + u) % 3
        first = jnp.where(rot == 0, cx, jnp.where(rot == 1, cz, cy))
        middle = jnp.where(rot == 0, cz, jnp.where(rot == 1, cy, cx))
        last = jnp.where(rot == 0, cy, jnp.where(rot == 1, cx, cz))
        return last, middle, first

    def own(u):
        last, middle, first = place(u, c, xx, z, y)
        return gath.at[u, c, last, middle, first]

    consts = [
        pltpu.make_async_copy(filt_hbm, filt, csem.at[0]),
        pltpu.make_async_copy(tab_hbm, tab, csem.at[1]),
        pltpu.make_async_copy(inv_hbm, inv, csem.at[2]),
    ]
    units = [
        pltpu.make_async_copy(pan_hbm.at[u // 2, pl.ds(8 * (u % 2), 8)], own(u), psem.at[u])
        for u in range(4)
    ]
    runs = [pltpu.make_async_copy(x_hbm.at[pl.ds(GROUP * i, GROUP)], x.at[pl.ds(GROUP * i, GROUP)], xsem.at[i])
            for i in range(4)]
    for copy in consts[:2] + units + runs + consts[2:]:
        copy.start()
    lax.fori_loop(1, DEVS, greet, 0)

    consts[0].wait()
    consts[1].wait()
    e, o = coefficients(filt[...])
    even[...] = e
    odd[...] = o

    for copy in units:
        copy.wait()
    pl.semaphore_wait(bar, DEVS - 1)

    def gather_start(phase):
        for u in range(4):
            last, middle, first = place(u, c, xx, z, y)
            axis = ((c * 4 + u) % 3 + phase) % 3
            stride = jnp.where(axis == 0, 2, jnp.where(axis == 1, 8, 32))
            at = jnp.where(axis == 0, xx, jnp.where(axis == 1, z, y))
            block = [gath.at[u, c, last, middle, first], gath.at[u, c, last, middle], gath.at[u, c, last]][phase]
            for step in (1, 3, 2):
                to = me + ((at + step) % 4 - at) * stride
                pltpu.make_async_remote_copy(
                    block, block, g_send.at[u, phase], g_recv.at[u, phase],
                    device_id=(to,), device_id_type=MESH,
                ).start()

    def gather_wait(phase):
        for u in range(4):
            three = pl.ds(0, 3)
            block = [gath.at[u, c, 0, 0, three], gath.at[u, c, 0, three], gath.at[u, c, three]][phase]
            whole = pltpu.make_async_remote_copy(
                block, block, g_send.at[u, phase], g_recv.at[u, phase],
                device_id=(partner,), device_id_type=MESH,
            )
            whole.wait_send()
            whole.wait_recv()

    def whiten(i):
        runs[i].wait()
        v, vt = (tab[0], tab[1]), (tab[2], tab[3])
        half = i // 2
        base = GROUP * (i % 2)
        rows = x[GROUP * i : GROUP * (i + 1)].reshape(GROUP * N, N)
        cols = dot3(split(rows), v)
        backs = []
        for g in range(GROUP):
            t = dot3(vt, split(cols[g * N : (g + 1) * N]))
            low, up = t[:HALF], t[HALF:]
            turned = jnp.concatenate(
                [
                    jnp.concatenate([up[:, HALF:], up[:, :HALF]], axis=1),
                    jnp.concatenate([low[:, HALF:], low[:, :HALF]], axis=1),
                ],
                axis=0,
            )
            backs.append(even[...] * t + odd[...] * turned)
        spread = dot3(split(jnp.concatenate(backs, axis=0)), vt)
        for g in range(GROUP):
            done = dot3(v, split(spread[g * N : (g + 1) * N]))
            for h in range(2):
                out[half, h, pl.ds(base + g, N, stride=8), :] = done[:, h * HALF : (h + 1) * HALF]

    def send_half(half):
        def send(k, carry):
            dx = k % 4
            dy = (dx + (k // 4) % 4) % 4
            dz = (dx + (k // 16) % 4) % 4
            d = ((((y + dy) % 4) * 4 + (z + dz) % 4) * 4 + (xx + dx) % 4) * 2 + (c + k // 64) % 2
            pltpu.make_async_remote_copy(
                out.at[half, :, pl.ds(pl.multiple_of(d * 16, 16), 16)], land.at[:, me, half],
                a_send.at[half], a_recv.at[half], device_id=(d,), device_id_type=MESH,
            ).start()
            return carry

        lax.fori_loop(1, DEVS, send, 0)
        return pltpu.make_async_copy(
            out.at[half, :, pl.ds(pl.multiple_of(me * 16, 16), 16)], land.at[:, me, half], lsem.at[half]
        )

    gather_start(0)
    whiten(0)
    gather_wait(0)
    gather_start(1)
    whiten(1)
    gather_wait(1)
    gather_start(2)
    local0 = send_half(0)
    local0.start()
    whiten(2)
    whiten(3)
    local1 = send_half(1)
    local1.start()
    gather_wait(2)

    swaps = []
    for u in range(4):
        block = gath.at[u, c]
        swap = pltpu.make_async_remote_copy(
            block, block, g_send.at[u, 3], g_recv.at[u, 3], device_id=(partner,), device_id_type=MESH
        )
        swap.start()
        swaps.append(swap)
    for swap in swaps:
        swap.wait_send()
        swap.wait_recv()
    consts[2].wait()

    def order(d, carry):
        cy, cz, cx, core = d // 32, (d // 8) % 4, (d // 2) % 4, d % 2
        for u in range(4):
            last, middle, first = place(u, core, cx, cz, cy)
            to = pl.ds(pl.multiple_of(d * 16 + 8 * (u % 2), 8), 8)
            pan[u // 2, to, :] = gath[u, core, last, middle, first]
        return carry

    lax.fori_loop(0, DEVS, order, 0)

    b0, b1 = split(inv[0]), split(inv[1])
    joined = dot3(split(pan[0, N : 2 * N, :]), b0)
    joined_parts = split(joined)
    cross = dot3(b1, joined_parts)

    def put(start, left, right):
        lh, ll = split(left)
        rh, rl = split(right)
        rows = pl.ds(start, N)
        gh[rows, :N] = lh
        gl[rows, :N] = ll
        gh[rows, N:] = rh
        gl[rows, N:] = rl

    put(0, inv[0], jnp.zeros((N, N), F32))
    put(N, -cross, inv[1])

    def combine(i, carry):
        start = pl.multiple_of(i * N, N)
        h1 = dot3(split(pan[1, pl.ds(start, N), :]), b1)
        h0 = dot3(split(pan[0, pl.ds(start, N), :]), b0) - dot3(split(h1), joined_parts)
        put(start, -h0, -h1)
        return carry

    lax.fori_loop(2, 8, combine, 0)
    outs = [
        pltpu.make_async_copy(gh, gh_hbm, gsem.at[0]),
        pltpu.make_async_copy(gl, gl_hbm, gsem.at[1]),
    ]
    for copy in outs:
        copy.start()
    for copy in outs:
        copy.wait()
    local0.wait()
    local1.wait()
    for half in range(2):
        rest = pl.ds(0, (DEVS - 1) * 16)
        whole = pltpu.make_async_remote_copy(
            out.at[half, :, rest], out.at[half, :, rest], a_send.at[half], a_recv.at[half],
            device_id=(partner,), device_id_type=MESH,
        )
        whole.wait_send()
        whole.wait_recv()


def front(runs_field, filter_t, block_inverses, factor_panels, table):
    anywhere = pl.BlockSpec(memory_space=pl.ANY)
    return pl.pallas_call(
        front_kernel,
        out_shape=(
            jax.ShapeDtypeStruct((2, DEVS, 2, 16, HALF), F32),
            jax.ShapeDtypeStruct((2048, 512), BF16),
            jax.ShapeDtypeStruct((2048, 512), BF16),
        ),
        in_specs=[anywhere] * 5,
        out_specs=(anywhere,) * 3,
        scratch_shapes=[
            pltpu.VMEM((16, N, N), F32),
            pltpu.VMEM((129, N), F32),
            pltpu.VMEM((2, N, N), F32),
            pltpu.VMEM((4, N, N), BF16),
            pltpu.VMEM((N, N), F32),
            pltpu.VMEM((N, N), F32),
            pltpu.VMEM((2, 2, 2048, HALF), F32),
            pltpu.VMEM((4, 2, 4, 4, 4, 8, N), F32),
            pltpu.VMEM((2, 2048, N), F32),
            pltpu.VMEM((2048, 512), BF16),
            pltpu.VMEM((2048, 512), BF16),
            pltpu.SemaphoreType.DMA((4,)),
            pltpu.SemaphoreType.DMA((3,)),
            pltpu.SemaphoreType.DMA((4,)),
            pltpu.SemaphoreType.DMA((2,)),
            pltpu.SemaphoreType.DMA((2,)),
            pltpu.SemaphoreType.DMA((2,)),
            pltpu.SemaphoreType.DMA((4, 4)),
            pltpu.SemaphoreType.DMA((4, 4)),
            pltpu.SemaphoreType.DMA((2,)),
        ],
        compiler_params=pltpu.CompilerParams(
            collective_id=0, has_side_effects=True, vmem_limit_bytes=56 << 20
        ),
        name="front",
    )(runs_field, filter_t, block_inverses, factor_panels, table)


def unpack(block):
    sources = block.shape[1]
    parts = []
    for row in range(2):
        for h in range(2):
            part = block[h, :, :, 8 * row : 8 * row + 8, :]
            parts.append(part.reshape(sources * 16, HALF))
    return jnp.concatenate(parts, axis=1)


def solve_kernel(top_ref, w_ref, gh_ref, gl_ref, o_ref, wh, wl):
    step = pl.program_id(0)

    @pl.when(step == 0)
    def _():
        high, low = split(unpack(top_ref))
        wh[...] = high
        wl[...] = low

    product = dot3((gh_ref[...], gl_ref[...]), (wh[...], wl[...]))
    rows = o_ref.shape[0]
    solved = step * rows < 512

    @pl.when(solved)
    def _():
        o_ref[...] = product

    @pl.when(jnp.logical_not(solved))
    def _():
        o_ref[...] = product + unpack(w_ref)


def solve(landed, gh, gl):
    rows = 256
    return pl.pallas_call(
        solve_kernel,
        grid=(2048 // rows,),
        out_shape=jax.ShapeDtypeStruct((2048, 512), F32),
        in_specs=[
            pl.BlockSpec((2, 32, 2, 16, HALF), lambda i: (0, 0, 0, 0, 0)),
            pl.BlockSpec((2, rows // 16, 2, 16, HALF), lambda i: (0, i, 0, 0, 0)),
            pl.BlockSpec((rows, 512), lambda i: (i, 0)),
            pl.BlockSpec((rows, 512), lambda i: (i, 0)),
        ],
        out_specs=pl.BlockSpec((rows, 512), lambda i: (i, 0)),
        scratch_shapes=[pltpu.VMEM((512, 512), BF16), pltpu.VMEM((512, 512), BF16)],
        compiler_params=pltpu.CompilerParams(vmem_limit_bytes=40 << 20),
        name="solve",
    )(landed, landed, gh, gl)


def per_device(runs_field, spectral_filter, block_inverses, factor_panels):
    landed, gh, gl = front(
        runs_field, spectral_filter.T, block_inverses, factor_panels, jnp.asarray(tables())
    )
    return solve(landed, gh, gl)


def solution(mesh):
    return jax.shard_map(
        per_device,
        mesh=mesh,
        in_specs=(P("dev", None, None), P(), P(), P(None, "dev", None)),
        out_specs=P(None, "dev"),
        check_vma=False,
    )
```

profile of v0, /device:TPU:1, one launch (start us, length us, event | category | flops | bytes accessed | tf_op | source)
XLA Modules:
  0.0 87.6 jit_solution(6199252568965483751)
XLA Ops:
  0.0 75.6 %front.1 = (f32[2,128,2,16,128]{4,3,2,1,0:T(8,128)}, bf16[2048,512]{1,0:T(8,128)(2,1)}, bf16[2048,512]{1,0:T(8,128)(2,1)}) custom-call(f32[16,256,256]{2,1,0:T(8,128)} %x_hbm.1, f32[129,256]{1,0:T(8,128)} %bitcast.1, f32[2,256,256]{2,1,0:T(8,128)} %inv_hbm.1, f32[2,16,256]{2,1,0:T(8,128)} %pan_hbm.1, bf16[4,256,256]{2,1,0:T(8,128)(2,1)} %constant.2.clone.tab_hbm), custom_call_target="tpu_custom_call" | custom-call | tf_op jit(solution)/shard_map/front/pallas_call | solution.py:276
  75.6 0.0 copy-start
  75.6 2.2 %copy-done = f32[2,128,2,16,128]{4,3,2,1,0:T(8,128)S(1)} copy-done((f32[2,128,2,16,128]{4,3,2,1,0:T(8,128)S(1)}, f32[2,128,2,16,128]{4,3,2,1,0:T(8,128)}, u32[]{:S(2)}) %copy-start) | copy-done | bytes 4194328
  77.8 0.0 copy-start.1
  77.8 1.6 %copy-done.1 = bf16[2048,512]{1,0:T(8,128)(2,1)S(1)} copy-done((bf16[2048,512]{1,0:T(8,128)(2,1)S(1)}, bf16[2048,512]{1,0:T(8,128)(2,1)}, u32[]{:S(2)}) %copy-start.1) | copy-done | bytes 2097176
  79.4 0.0 copy-start.2
  79.4 1.6 %copy-done.2 = bf16[2048,512]{1,0:T(8,128)(2,1)S(1)} copy-done((bf16[2048,512]{1,0:T(8,128)(2,1)S(1)}, bf16[2048,512]{1,0:T(8,128)(2,1)}, u32[]{:S(2)}) %copy-start.2) | copy-done | bytes 2097176
  81.0 6.7 %solve.1 = f32[2048,512]{1,0:T(8,128)} custom-call(f32[2,128,2,16,128]{4,3,2,1,0:T(8,128)S(1)} %copy-done, f32[2,128,2,16,128]{4,3,2,1,0:T(8,128)S(1)} %copy-done, bf16[2048,512]{1,0:T(8,128)(2,1)S(1)} %copy-done.1, bf16[2048,512]{1,0:T(8,128)(2,1)S(1)} %copy-done.2), custom_call_target="tpu_custom_call" | custom-call | tf_op jit(solution)/shard_map/solve/pallas_call | solution.py:348
Async XLA Ops:
  75.6 2.2 %copy-start = (f32[2,128,2,16,128]{4,3,2,1,0:T(8,128)S(1)}, f32[2,128,2,16,128]{4,3,2,1,0:T(8,128)}, u32[]{:S(2)}) copy-start(f32[2,128,2,16,128]{4,3,2,1,0:T(8,128)} %get-tuple-element.8.top_ref.w_ref) | copy-start | bytes 12582916
  77.8 1.6 %copy-start.1 = (bf16[2048,512]{1,0:T(8,128)(2,1)S(1)}, bf16[2048,512]{1,0:T(8,128)(2,1)}, u32[]{:S(2)}) copy-start(bf16[2048,512]{1,0:T(8,128)(2,1)} %get-tuple-element.9.gh_ref) | copy-start | bytes 6291460
  79.4 1.6 %copy-start.2 = (bf16[2048,512]{1,0:T(8,128)(2,1)S(1)}, bf16[2048,512]{1,0:T(8,128)(2,1)}, u32[]{:S(2)}) copy-start(bf16[2048,512]{1,0:T(8,128)(2,1)} %get-tuple-element.10.gl_ref) | copy-start | bytes 6291460
where the time goes:
time: 87.8 us; the launch traced here: 87.6 us
  Pallas kernels  82.3 us (94%)
  local copies, waits for them, and re-layouts  5.36 us (6%)
    pallas_call x1, Pallas kernels, front(): pl.pallas_call(front_kernel, out_shape=(jax.ShapeDtypeStruct((2, DEVS, 2,...  75.6 us
    pallas_call x1, Pallas kernels, solve(): pl.pallas_call(solve_kernel, grid=(2048 // rows,), out_shape=jax.ShapeDty...  6.66 us
    unnamed x6, local copies, waits for them, and re-layouts  5.36 us

commit v1 on v0

--- a/solution.py
+++ b/solution.py
@@ -72,9 +72,9 @@
 
 
 def front_kernel(
-    x_hbm, filt_hbm, inv_hbm, pan_hbm, tab_hbm, land, gh_hbm, gl_hbm,
-    x, filt, inv, tab, even, odd, out, gath, pan, gh, gl,
-    xsem, csem, psem, gsem, a_send, a_recv, g_send, g_recv, lsem,
+    x_hbm, filt_hbm, inv_hbm, pan_hbm, tab_hbm, o_hbm,
+    x, filt, inv, tab, even, odd, out, land, gath, pan, factor, acc, wh, wl,
+    xsem, csem, psem, osem, a_send, a_recv, g_send, g_recv, lsem,
 ):
     me = lax.axis_index("dev")
     y, z, xx, c = me // 32, (me // 8) % 4, (me // 2) % 4, me % 2
@@ -111,12 +111,6 @@
         copy.start()
     lax.fori_loop(1, DEVS, greet, 0)
 
-    consts[0].wait()
-    consts[1].wait()
-    e, o = coefficients(filt[...])
-    even[...] = e
-    odd[...] = o
-
     for copy in units:
         copy.wait()
     pl.semaphore_wait(bar, DEVS - 1)
@@ -149,8 +143,6 @@
     def whiten(i):
         runs[i].wait()
         v, vt = (tab[0], tab[1]), (tab[2], tab[3])
-        half = i // 2
-        base = GROUP * (i % 2)
         rows = x[GROUP * i : GROUP * (i + 1)].reshape(GROUP * N, N)
         cols = dot3(split(rows), v)
         backs = []
@@ -169,38 +161,54 @@
         for g in range(GROUP):
             done = dot3(v, split(spread[g * N : (g + 1) * N]))
             for h in range(2):
-                out[half, h, pl.ds(base + g, N, stride=8), :] = done[:, h * HALF : (h + 1) * HALF]
-
-    def send_half(half):
+                out[i, h, pl.ds(g, N, stride=GROUP), :] = done[:, h * HALF : (h + 1) * HALF]
+
+    def send_part(part):
         def send(k, carry):
             dx = k % 4
             dy = (dx + (k // 4) % 4) % 4
             dz = (dx + (k // 16) % 4) % 4
             d = ((((y + dy) % 4) * 4 + (z + dz) % 4) * 4 + (xx + dx) % 4) * 2 + (c + k // 64) % 2
             pltpu.make_async_remote_copy(
-                out.at[half, :, pl.ds(pl.multiple_of(d * 16, 16), 16)], land.at[:, me, half],
-                a_send.at[half], a_recv.at[half], device_id=(d,), device_id_type=MESH,
+                out.at[part, :, pl.ds(pl.multiple_of(d * 8, 8), 8)], land.at[:, part, me],
+                a_send.at[part], a_recv.at[part], device_id=(d,), device_id_type=MESH,
             ).start()
             return carry
 
         lax.fori_loop(1, DEVS, send, 0)
-        return pltpu.make_async_copy(
-            out.at[half, :, pl.ds(pl.multiple_of(me * 16, 16), 16)], land.at[:, me, half], lsem.at[half]
+        local = pltpu.make_async_copy(
+            out.at[part, :, pl.ds(pl.multiple_of(me * 8, 8), 8)], land.at[:, part, me], lsem.at[part]
         )
+        local.start()
+        return local
+
+    def arrived(part):
+        locals_[part].wait()
+        rest = pl.ds(0, (DEVS - 1) * 8)
+        whole = pltpu.make_async_remote_copy(
+            out.at[part, :, rest], out.at[part, :, rest], a_send.at[part], a_recv.at[part],
+            device_id=(partner,), device_id_type=MESH,
+        )
+        whole.wait_send()
+        whole.wait_recv()
 
     gather_start(0)
+    consts[0].wait()
+    consts[1].wait()
+    e, o = coefficients(filt[...])
+    even[...] = e
+    odd[...] = o
     whiten(0)
     gather_wait(0)
     gather_start(1)
+    locals_ = [send_part(0)]
     whiten(1)
     gather_wait(1)
     gather_start(2)
-    local0 = send_half(0)
-    local0.start()
-    whiten(2)
-    whiten(3)
-    local1 = send_half(1)
-    local1.start()
+    locals_.append(send_part(1))
+    for part in (2, 3):
+        whiten(part)
+        locals_.append(send_part(part))
     gather_wait(2)
 
     swaps = []
@@ -231,14 +239,19 @@
     joined_parts = split(joined)
     cross = dot3(b1, joined_parts)
 
+    row = lax.broadcasted_iota(jnp.int32, (N, N), 0)
+    col = lax.broadcasted_iota(jnp.int32, (N, N), 1)
+    shuffle = (col == (row // 8 % 2) * HALF + row // 16 * 8 + row % 8).astype(BF16)
+
     def put(start, left, right):
-        lh, ll = split(left)
-        rh, rl = split(right)
         rows = pl.ds(start, N)
-        gh[rows, :N] = lh
-        gl[rows, :N] = ll
-        gh[rows, N:] = rh
-        gl[rows, N:] = rl
+        for side, value in enumerate((left, right)):
+            for level, part in enumerate(split(value)):
+                moved = dot(part, shuffle).astype(BF16)
+                for half in range(2):
+                    factor[half, level, rows, HALF * side : HALF * (side + 1)] = moved[
+                        :, HALF * half : HALF * (half + 1)
+                    ]
 
     put(0, inv[0], jnp.zeros((N, N), F32))
     put(N, -cross, inv[1])
@@ -251,37 +264,63 @@
         return carry
 
     lax.fori_loop(2, 8, combine, 0)
-    outs = [
-        pltpu.make_async_copy(gh, gh_hbm, gsem.at[0]),
-        pltpu.make_async_copy(gl, gl_hbm, gsem.at[1]),
-    ]
-    for copy in outs:
-        copy.start()
-    for copy in outs:
-        copy.wait()
-    local0.wait()
-    local1.wait()
-    for half in range(2):
-        rest = pl.ds(0, (DEVS - 1) * 16)
-        whole = pltpu.make_async_remote_copy(
-            out.at[half, :, rest], out.at[half, :, rest], a_send.at[half], a_recv.at[half],
-            device_id=(partner,), device_id_type=MESH,
-        )
-        whole.wait_send()
-        whole.wait_recv()
+
+    def rows_of(half, start, sources):
+        lower = lax.broadcasted_iota(jnp.int32, (sources, 8, HALF), 1) < GROUP
+        columns = [None] * 4
+        for h in range(2):
+            a = land[h, 2 * half, pl.ds(start, sources)]
+            b = land[h, 2 * half + 1, pl.ds(start, sources)]
+            columns[h] = jnp.where(lower, a, pltpu.roll(b, GROUP, 1))
+            columns[2 + h] = jnp.where(lower, pltpu.roll(a, GROUP, 1), b)
+        return jnp.concatenate(columns, axis=2)
+
+    def multiply(half):
+        high, low = split(rows_of(half, 0, 32).reshape(N, 512))
+        wh[...] = high
+        wl[...] = low
+
+        def chunk(i, own):
+            rows = pl.ds(pl.multiple_of(i * N, N), N)
+            product = dot3((factor[half, 0, rows, :], factor[half, 1, rows, :]), (wh[...], wl[...]))
+            if own:
+                mine = rows_of(half, i * 16, 16)
+                none = jnp.zeros_like(mine)
+                both = [mine, none] if half == 0 else [none, mine]
+                product = product + jnp.stack(both, axis=1).reshape(N, 512)
+            if half == 0:
+                acc[rows, :] = product
+            else:
+                acc[rows, :] = acc[rows, :] + product
+                pltpu.make_async_copy(acc.at[rows], o_hbm.at[rows], osem.at[i]).start()
+
+        for i in range(2):
+            chunk(i, False)
+
+        def later(i, carry):
+            chunk(i, True)
+            return carry
+
+        lax.fori_loop(2, 8, later, 0)
+
+    arrived(0)
+    arrived(1)
+    multiply(0)
+    arrived(2)
+    arrived(3)
+    multiply(1)
+    for i in range(8):
+        rows = pl.ds(i * N, N)
+        pltpu.make_async_copy(acc.at[rows], o_hbm.at[rows], osem.at[i]).wait()
 
 
 def front(runs_field, filter_t, block_inverses, factor_panels, table):
     anywhere = pl.BlockSpec(memory_space=pl.ANY)
     return pl.pallas_call(
         front_kernel,
-        out_shape=(
-            jax.ShapeDtypeStruct((2, DEVS, 2, 16, HALF), F32),
-            jax.ShapeDtypeStruct((2048, 512), BF16),
-            jax.ShapeDtypeStruct((2048, 512), BF16),
-        ),
+        out_shape=jax.ShapeDtypeStruct((2048, 512), F32),
         in_specs=[anywhere] * 5,
-        out_specs=(anywhere,) * 3,
+        out_specs=anywhere,
         scratch_shapes=[
             pltpu.VMEM((16, N, N), F32),
             pltpu.VMEM((129, N), F32),
@@ -289,20 +328,23 @@
             pltpu.VMEM((4, N, N), BF16),
             pltpu.VMEM((N, N), F32),
             pltpu.VMEM((N, N), F32),
-            pltpu.VMEM((2, 2, 2048, HALF), F32),
+            pltpu.VMEM((4, 2, 1024, HALF), F32),
+            pltpu.VMEM((2, 4, DEVS, 8, HALF), F32),
             pltpu.VMEM((4, 2, 4, 4, 4, 8, N), F32),
             pltpu.VMEM((2, 2048, N), F32),
-            pltpu.VMEM((2048, 512), BF16),
-            pltpu.VMEM((2048, 512), BF16),
+            pltpu.VMEM((2, 2, 2048, N), BF16),
+            pltpu.VMEM((2048, 512), F32),
+            pltpu.VMEM((N, 512), BF16),
+            pltpu.VMEM((N, 512), BF16),
             pltpu.SemaphoreType.DMA((4,)),
             pltpu.SemaphoreType.DMA((3,)),
             pltpu.SemaphoreType.DMA((4,)),
-            pltpu.SemaphoreType.DMA((2,)),
-            pltpu.SemaphoreType.DMA((2,)),
-            pltpu.SemaphoreType.DMA((2,)),
+            pltpu.SemaphoreType.DMA((8,)),
+            pltpu.SemaphoreType.DMA((4,)),
+            pltpu.SemaphoreType.DMA((4,)),
             pltpu.SemaphoreType.DMA((4, 4)),
             pltpu.SemaphoreType.DMA((4, 4)),
-            pltpu.SemaphoreType.DMA((2,)),
+            pltpu.SemaphoreType.DMA((4,)),
         ],
         compiler_params=pltpu.CompilerParams(
             collective_id=0, has_side_effects=True, vmem_limit_bytes=56 << 20
@@ -311,62 +353,8 @@
     )(runs_field, filter_t, block_inverses, factor_panels, table)
 
 
-def unpack(block):
-    sources = block.shape[1]
-    parts = []
-    for row in range(2):
-        for h in range(2):
-            part = block[h, :, :, 8 * row : 8 * row + 8, :]
-            parts.append(part.reshape(sources * 16, HALF))
-    return jnp.concatenate(parts, axis=1)
-
-
-def solve_kernel(top_ref, w_ref, gh_ref, gl_ref, o_ref, wh, wl):
-    step = pl.program_id(0)
-
-    @pl.when(step == 0)
-    def _():
-        high, low = split(unpack(top_ref))
-        wh[...] = high
-        wl[...] = low
-
-    product = dot3((gh_ref[...], gl_ref[...]), (wh[...], wl[...]))
-    rows = o_ref.shape[0]
-    solved = step * rows < 512
-
-    @pl.when(solved)
-    def _():
-        o_ref[...] = product
-
-    @pl.when(jnp.logical_not(solved))
-    def _():
-        o_ref[...] = product + unpack(w_ref)
-
-
-def solve(landed, gh, gl):
-    rows = 256
-    return pl.pallas_call(
-        solve_kernel,
-        grid=(2048 // rows,),
-        out_shape=jax.ShapeDtypeStruct((2048, 512), F32),
-        in_specs=[
-            pl.BlockSpec((2, 32, 2, 16, HALF), lambda i: (0, 0, 0, 0, 0)),
-            pl.BlockSpec((2, rows // 16, 2, 16, HALF), lambda i: (0, i, 0, 0, 0)),
-            pl.BlockSpec((rows, 512), lambda i: (i, 0)),
-            pl.BlockSpec((rows, 512), lambda i: (i, 0)),
-        ],
-        out_specs=pl.BlockSpec((rows, 512), lambda i: (i, 0)),
-        scratch_shapes=[pltpu.VMEM((512, 512), BF16), pltpu.VMEM((512, 512), BF16)],
-        compiler_params=pltpu.CompilerParams(vmem_limit_bytes=40 << 20),
-        name="solve",
-    )(landed, landed, gh, gl)
-
-
 def per_device(runs_field, spectral_filter, block_inverses, factor_panels):
-    landed, gh, gl = front(
-        runs_field, spectral_filter.T, block_inverses, factor_panels, jnp.asarray(tables())
-    )
-    return solve(landed, gh, gl)
+    return front(runs_field, spectral_filter.T, block_inverses, factor_panels, jnp.asarray(tables()))
 
 
 def solution(mesh):

time: 87.8 us -> 82.3 us (0.937)
  Pallas kernels: 82.3 us -> 77.5 us
    pallas_call x2 -> x1, Pallas kernels: 82.3 us -> 77.5 us  [front(): pl.pallas_call(front_kernel, out_shape=jax.ShapeDtypeStruct((2048, 512),...]
    unnamed x6 -> x1, local copies, waits for them, and re-layouts: 5.36 us -> 4.64 us
where the time goes in v1:
time: 82.3 us; the launch traced here: 82.1 us
  Pallas kernels  77.5 us (94%)
  local copies, waits for them, and re-layouts  4.64 us (6%)
    pallas_call x1, Pallas kernels, front(): pl.pallas_call(front_kernel, out_shape=jax.ShapeDtypeStruct((2048, 512),...  77.5 us
    unnamed x1, local copies, waits for them, and re-layouts  4.64 us

profile of v1, /device:TPU:1, one launch (start us, length us, event | category | flops | bytes accessed | tf_op | source)
XLA Modules:
  0.0 82.1 jit_solution(11401746736987744759)
XLA Ops:
  0.0 77.5 %front.1 = f32[2048,512]{1,0:T(8,128)} custom-call(f32[16,256,256]{2,1,0:T(8,128)} %x_hbm.1, f32[129,256]{1,0:T(8,128)} %bitcast.1, f32[2,256,256]{2,1,0:T(8,128)} %inv_hbm.1, f32[2,16,256]{2,1,0:T(8,128)} %pan_hbm.1, bf16[4,256,256]{2,1,0:T(8,128)(2,1)} %constant.2.clone.tab_hbm), custom_call_target="tpu_custom_call" | custom-call | tf_op jit(solution)/shard_map/front/pallas_call | solution.py:319
  77.5 4.6 %copy.7 = f32[2048,512]{1,0:T(8,128)} copy(f32[2048,512]{1,0:T(8,128)} %front.1) | data formatting | bytes 8388608

commit v2 on v1

--- a/solution.py
+++ b/solution.py
@@ -72,9 +72,9 @@
 
 
 def front_kernel(
-    x_hbm, filt_hbm, inv_hbm, pan_hbm, tab_hbm, o_hbm,
-    x, filt, inv, tab, even, odd, out, land, gath, pan, factor, acc, wh, wl,
-    xsem, csem, psem, osem, a_send, a_recv, g_send, g_recv, lsem,
+    x_hbm, filt_hbm, inv_hbm, pan_hbm, tab_hbm, acc,
+    x, filt, inv, tab, even, odd, out, land, gath, pan, factor, wh, wl,
+    xsem, csem, psem, a_send, a_recv, g_send, g_recv, lsem,
 ):
     me = lax.axis_index("dev")
     y, z, xx, c = me // 32, (me // 8) % 4, (me // 2) % 4, me % 2
@@ -111,18 +111,23 @@
         copy.start()
     lax.fori_loop(1, DEVS, greet, 0)
 
-    for copy in units:
-        copy.wait()
-    pl.semaphore_wait(bar, DEVS - 1)
-
     def gather_start(phase):
         for u in range(4):
             last, middle, first = place(u, c, xx, z, y)
-            axis = ((c * 4 + u) % 3 + phase) % 3
+            axis = ((c * 4 + u) % 3 + min(phase, 2)) % 3
             stride = jnp.where(axis == 0, 2, jnp.where(axis == 1, 8, 32))
             at = jnp.where(axis == 0, xx, jnp.where(axis == 1, z, y))
-            block = [gath.at[u, c, last, middle, first], gath.at[u, c, last, middle], gath.at[u, c, last]][phase]
-            for step in (1, 3, 2):
+            if phase < 2:
+                block = [gath.at[u, c, last, middle, first], gath.at[u, c, last, middle]][phase]
+                sends = [(1, block), (3, block), (2, block)]
+            elif phase == 2:
+                sends = [(1, gath.at[u, c, last]), (3, gath.at[u, c, last])]
+            else:
+                sends = [
+                    (1, gath.at[u, c, (last + 3) % 4, pl.ds(0, 2)]),
+                    (3, gath.at[u, c, (last + 1) % 4, pl.ds(2, 2)]),
+                ]
+            for step, block in sends:
                 to = me + ((at + step) % 4 - at) * stride
                 pltpu.make_async_remote_copy(
                     block, block, g_send.at[u, phase], g_recv.at[u, phase],
@@ -132,7 +137,12 @@
     def gather_wait(phase):
         for u in range(4):
             three = pl.ds(0, 3)
-            block = [gath.at[u, c, 0, 0, three], gath.at[u, c, 0, three], gath.at[u, c, three]][phase]
+            block = [
+                gath.at[u, c, 0, 0, three],
+                gath.at[u, c, 0, three],
+                gath.at[u, c, pl.ds(0, 2)],
+                gath.at[u, c, 0],
+            ][phase]
             whole = pltpu.make_async_remote_copy(
                 block, block, g_send.at[u, phase], g_recv.at[u, phase],
                 device_id=(partner,), device_id_type=MESH,
@@ -163,7 +173,7 @@
             for h in range(2):
                 out[i, h, pl.ds(g, N, stride=GROUP), :] = done[:, h * HALF : (h + 1) * HALF]
 
-    def send_part(part):
+    def send_part(part, low=1, high=DEVS):
         def send(k, carry):
             dx = k % 4
             dy = (dx + (k // 4) % 4) % 4
@@ -175,15 +185,15 @@
             ).start()
             return carry
 
-        lax.fori_loop(1, DEVS, send, 0)
-        local = pltpu.make_async_copy(
+        lax.fori_loop(low, high, send, 0)
+
+    def keep_part(part):
+        return pltpu.make_async_copy(
             out.at[part, :, pl.ds(pl.multiple_of(me * 8, 8), 8)], land.at[:, part, me], lsem.at[part]
         )
-        local.start()
-        return local
 
     def arrived(part):
-        locals_[part].wait()
+        keep_part(part).wait()
         rest = pl.ds(0, (DEVS - 1) * 8)
         whole = pltpu.make_async_remote_copy(
             out.at[part, :, rest], out.at[part, :, rest], a_send.at[part], a_recv.at[part],
@@ -192,30 +202,40 @@
         whole.wait_send()
         whole.wait_recv()
 
-    gather_start(0)
     consts[0].wait()
     consts[1].wait()
     e, o = coefficients(filt[...])
     even[...] = e
     odd[...] = o
     whiten(0)
+    for copy in units:
+        copy.wait()
+    pl.semaphore_wait(bar, DEVS - 1)
+    gather_start(0)
+    send_part(0, 1, 12)
+    whiten(1)
     gather_wait(0)
     gather_start(1)
-    locals_ = [send_part(0)]
-    whiten(1)
+    send_part(0, 12)
+    whiten(2)
     gather_wait(1)
     gather_start(2)
-    locals_.append(send_part(1))
-    for part in (2, 3):
-        whiten(part)
-        locals_.append(send_part(part))
+    send_part(1, 1, 24)
+    whiten(3)
     gather_wait(2)
+    gather_start(3)
+    send_part(1, 24)
+    send_part(2)
+    send_part(3)
+    for part in range(4):
+        keep_part(part).start()
+    gather_wait(3)
 
     swaps = []
     for u in range(4):
         block = gath.at[u, c]
         swap = pltpu.make_async_remote_copy(
-            block, block, g_send.at[u, 3], g_recv.at[u, 3], device_id=(partner,), device_id_type=MESH
+            block, block, g_send.at[u, 4], g_recv.at[u, 4], device_id=(partner,), device_id_type=MESH
         )
         swap.start()
         swaps.append(swap)
@@ -292,7 +312,6 @@
                 acc[rows, :] = product
             else:
                 acc[rows, :] = acc[rows, :] + product
-                pltpu.make_async_copy(acc.at[rows], o_hbm.at[rows], osem.at[i]).start()
 
         for i in range(2):
             chunk(i, False)
@@ -309,18 +328,15 @@
     arrived(2)
     arrived(3)
     multiply(1)
-    for i in range(8):
-        rows = pl.ds(i * N, N)
-        pltpu.make_async_copy(acc.at[rows], o_hbm.at[rows], osem.at[i]).wait()
 
 
 def front(runs_field, filter_t, block_inverses, factor_panels, table):
     anywhere = pl.BlockSpec(memory_space=pl.ANY)
     return pl.pallas_call(
         front_kernel,
-        out_shape=jax.ShapeDtypeStruct((2048, 512), F32),
+        out_shape=pltpu.VMEM((2048, 512), F32),
         in_specs=[anywhere] * 5,
-        out_specs=anywhere,
+        out_specs=pl.BlockSpec(memory_space=pltpu.VMEM),
         scratch_shapes=[
             pltpu.VMEM((16, N, N), F32),
             pltpu.VMEM((129, N), F32),
@@ -333,21 +349,19 @@
             pltpu.VMEM((4, 2, 4, 4, 4, 8, N), F32),
             pltpu.VMEM((2, 2048, N), F32),
             pltpu.VMEM((2, 2, 2048, N), BF16),
-            pltpu.VMEM((2048, 512), F32),
             pltpu.VMEM((N, 512), BF16),
             pltpu.VMEM((N, 512), BF16),
             pltpu.SemaphoreType.DMA((4,)),
             pltpu.SemaphoreType.DMA((3,)),
             pltpu.SemaphoreType.DMA((4,)),
-            pltpu.SemaphoreType.DMA((8,)),
-            pltpu.SemaphoreType.DMA((4,)),
-            pltpu.SemaphoreType.DMA((4,)),
-            pltpu.SemaphoreType.DMA((4, 4)),
-            pltpu.SemaphoreType.DMA((4, 4)),
+            pltpu.SemaphoreType.DMA((4,)),
+            pltpu.SemaphoreType.DMA((4,)),
+            pltpu.SemaphoreType.DMA((4, 5)),
+            pltpu.SemaphoreType.DMA((4, 5)),
             pltpu.SemaphoreType.DMA((4,)),
         ],
         compiler_params=pltpu.CompilerParams(
-            collective_id=0, has_side_effects=True, vmem_limit_bytes=56 << 20
+            collective_id=0, has_side_effects=True, vmem_limit_bytes=58 << 20
         ),
         name="front",
     )(runs_field, filter_t, block_inverses, factor_panels, table)

time: 82.3 us -> 77.5 us (0.942)
  local copies, waits for them, and re-layouts: 4.64 us -> 2.02 us
  Pallas kernels: 77.5 us -> 75.4 us
    unnamed x1, local copies, waits for them, and re-layouts: 4.64 us -> 2.02 us
    pallas_call x1, Pallas kernels: 77.5 us -> 75.4 us  [front(): pl.pallas_call(front_kernel, out_shape=pltpu.VMEM((2048, 512), F32), in_s...]
where the time goes in v2:
time: 77.5 us; the launch traced here: 77.4 us
  Pallas kernels  75.4 us (97%)
  local copies, waits for them, and re-layouts  2.02 us (3%)
    pallas_call x1, Pallas kernels, front(): pl.pallas_call(front_kernel, out_shape=pltpu.VMEM((2048, 512), F32), in_s...  75.4 us
    unnamed x1, local copies, waits for them, and re-layouts  2.02 us

profile of v2, /device:TPU:1, one launch (start us, length us, event | category | flops | bytes accessed | tf_op | source)
XLA Modules:
  0.0 77.4 jit_solution(827342593122789054)
XLA Ops:
  0.0 75.4 %front.1 = f32[2048,512]{1,0:T(8,128)S(1)} custom-call(f32[16,256,256]{2,1,0:T(8,128)} %x_hbm.1, f32[129,256]{1,0:T(8,128)} %bitcast.1, f32[2,256,256]{2,1,0:T(8,128)} %inv_hbm.1, f32[2,16,256]{2,1,0:T(8,128)} %pan_hbm.1, bf16[4,256,256]{2,1,0:T(8,128)(2,1)} %constant.2.clone.tab_hbm), custom_call_target="tpu_custom_call" | custom-call | tf_op jit(solution)/shard_map/front/pallas_call | solution.py:335
  75.4 2.0 %copy.7 = f32[2048,512]{1,0:T(8,128)} copy(f32[2048,512]{1,0:T(8,128)S(1)} %front.1) | data formatting | bytes 8388608

commit v3 on v2

--- a/solution.py
+++ b/solution.py
@@ -1,3 +1,4 @@
+import functools
 import math
 
 import jax
@@ -220,11 +221,11 @@
     whiten(2)
     gather_wait(1)
     gather_start(2)
-    send_part(1, 1, 24)
+    send_part(1, 1, 36)
     whiten(3)
     gather_wait(2)
     gather_start(3)
-    send_part(1, 24)
+    send_part(1, 36)
     send_part(2)
     send_part(3)
     for part in range(4):
@@ -239,20 +240,22 @@
         )
         swap.start()
         swaps.append(swap)
-    for swap in swaps:
-        swap.wait_send()
-        swap.wait_recv()
-    consts[2].wait()
-
-    def order(d, carry):
-        cy, cz, cx, core = d // 32, (d // 8) % 4, (d // 2) % 4, d % 2
+
+    def order(e, carry, core):
+        cy, cz, cx = e // 16, (e // 4) % 4, e % 4
+        d = e * 2 + core
         for u in range(4):
             last, middle, first = place(u, core, cx, cz, cy)
             to = pl.ds(pl.multiple_of(d * 16 + 8 * (u % 2), 8), 8)
             pan[u // 2, to, :] = gath[u, core, last, middle, first]
         return carry
 
-    lax.fori_loop(0, DEVS, order, 0)
+    lax.fori_loop(0, DEVS // 2, functools.partial(order, core=c), 0)
+    for swap in swaps:
+        swap.wait_send()
+        swap.wait_recv()
+    consts[2].wait()
+    lax.fori_loop(0, DEVS // 2, functools.partial(order, core=1 - c), 0)
 
     b0, b1 = split(inv[0]), split(inv[1])
     joined = dot3(split(pan[0, N : 2 * N, :]), b0)
@@ -301,26 +304,27 @@
         wl[...] = low
 
         def chunk(i, own):
-            rows = pl.ds(pl.multiple_of(i * N, N), N)
-            product = dot3((factor[half, 0, rows, :], factor[half, 1, rows, :]), (wh[...], wl[...]))
+            rows = pl.ds(i * 512, 512)
+            high, low = factor[half, 0, rows, :], factor[half, 1, rows, :]
+            product = dot(jnp.concatenate([high, low, high], axis=1), jnp.concatenate([wh[...], wh[...], wl[...]], axis=0))
             if own:
-                mine = rows_of(half, i * 16, 16)
+                mine = rows_of(half, i * 32, 32)
                 none = jnp.zeros_like(mine)
                 both = [mine, none] if half == 0 else [none, mine]
-                product = product + jnp.stack(both, axis=1).reshape(N, 512)
+                product = product + jnp.stack(both, axis=1).reshape(512, 512)
             if half == 0:
                 acc[rows, :] = product
             else:
                 acc[rows, :] = acc[rows, :] + product
 
-        for i in range(2):
-            chunk(i, False)
+        chunk(0, False)
 
         def later(i, carry):
             chunk(i, True)
             return carry
 
-        lax.fori_loop(2, 8, later, 0)
+        for i in range(1, 4):
+            later(i, 0)
 
     arrived(0)
     arrived(1)

time: 77.5 us -> 75.8 us (0.978)
  Pallas kernels: 75.4 us -> 73.7 us
    pallas_call x1, Pallas kernels: 75.4 us -> 73.7 us  [front(): pl.pallas_call(front_kernel, out_shape=pltpu.VMEM((2048, 512), F32), in_s...]
where the time goes in v3:
time: 75.8 us; the launch traced here: 75.7 us
  Pallas kernels  73.7 us (97%)
  local copies, waits for them, and re-layouts  2.02 us (3%)
    pallas_call x1, Pallas kernels, front(): pl.pallas_call(front_kernel, out_shape=pltpu.VMEM((2048, 512), F32), in_s...  73.7 us
    unnamed x1, local copies, waits for them, and re-layouts  2.02 us

profile of v3, /device:TPU:1, one launch (start us, length us, event | category | flops | bytes accessed | tf_op | source)
XLA Modules:
  0.0 75.7 jit_solution(8995534110700036727)
XLA Ops:
  0.0 73.7 %front.1 = f32[2048,512]{1,0:T(8,128)S(1)} custom-call(f32[16,256,256]{2,1,0:T(8,128)} %x_hbm.1, f32[129,256]{1,0:T(8,128)} %bitcast.1, f32[2,256,256]{2,1,0:T(8,128)} %inv_hbm.1, f32[2,16,256]{2,1,0:T(8,128)} %pan_hbm.1, bf16[4,256,256]{2,1,0:T(8,128)(2,1)} %constant.2.clone.tab_hbm), custom_call_target="tpu_custom_call" | custom-call | tf_op jit(solution)/shard_map/front/pallas_call | solution.py:339
  73.7 2.0 %copy.7 = f32[2048,512]{1,0:T(8,128)} copy(f32[2048,512]{1,0:T(8,128)S(1)} %front.1) | data formatting | bytes 8388608

commit v4 on v3

--- a/solution.py
+++ b/solution.py
@@ -267,7 +267,7 @@
     shuffle = (col == (row // 8 % 2) * HALF + row // 16 * 8 + row % 8).astype(BF16)
 
     def put(start, left, right):
-        rows = pl.ds(start, N)
+        rows = pl.ds(start, left.shape[0])
         for side, value in enumerate((left, right)):
             for level, part in enumerate(split(value)):
                 moved = dot(part, shuffle).astype(BF16)
@@ -280,13 +280,14 @@
     put(N, -cross, inv[1])
 
     def combine(i, carry):
-        start = pl.multiple_of(i * N, N)
-        h1 = dot3(split(pan[1, pl.ds(start, N), :]), b1)
-        h0 = dot3(split(pan[0, pl.ds(start, N), :]), b0) - dot3(split(h1), joined_parts)
+        start = i * 512
+        h1 = dot3(split(pan[1, pl.ds(start, 512), :]), b1)
+        h0 = dot3(split(pan[0, pl.ds(start, 512), :]), b0) - dot3(split(h1), joined_parts)
         put(start, -h0, -h1)
         return carry
 
-    lax.fori_loop(2, 8, combine, 0)
+    for i in range(1, 4):
+        combine(i, 0)
 
     def rows_of(half, start, sources):
         lower = lax.broadcasted_iota(jnp.int32, (sources, 8, HALF), 1) < GROUP

time: 75.8 us -> 75.8 us (level)
  no operation moved by 1% of the time
where the time goes in v4:
time: 75.8 us; the launch traced here: 75.7 us
  Pallas kernels  73.7 us (97%)
  local copies, waits for them, and re-layouts  2.02 us (3%)
    pallas_call x1, Pallas kernels, front(): pl.pallas_call(front_kernel, out_shape=pltpu.VMEM((2048, 512), F32), in_s...  73.7 us
    unnamed x1, local copies, waits for them, and re-layouts  2.02 us

profile of v4, /device:TPU:1, one launch (start us, length us, event | category | flops | bytes accessed | tf_op | source)
XLA Modules:
  0.0 75.7 jit_solution(16506300664857678928)
XLA Ops:
  0.0 73.7 %front.1 = f32[2048,512]{1,0:T(8,128)S(1)} custom-call(f32[16,256,256]{2,1,0:T(8,128)} %x_hbm.1, f32[129,256]{1,0:T(8,128)} %bitcast.1, f32[2,256,256]{2,1,0:T(8,128)} %inv_hbm.1, f32[2,16,256]{2,1,0:T(8,128)} %pan_hbm.1, bf16[4,256,256]{2,1,0:T(8,128)(2,1)} %constant.2.clone.tab_hbm), custom_call_target="tpu_custom_call" | custom-call | tf_op jit(solution)/shard_map/front/pallas_call | solution.py:340
  73.7 2.0 %copy.7 = f32[2048,512]{1,0:T(8,128)} copy(f32[2048,512]{1,0:T(8,128)S(1)} %front.1) | data formatting | bytes 8388608
